TPU v7x, 256 devices: a whole 4x4x8 slice. The times are simulated.
256 devices in a mesh: grp: 32 (over z_lo, y, core), tp: 8 (over x, z_hi).
Axes of the slice: x: 4, y: 4, z: 8 (z_hi: 2, z_lo: 4; z = z_hi * 4 + z_lo), core: 2. Of those that a mesh axis runs over, the one named last changes fastest.
Arguments:
- latents: bfloat16 [32768, 2048], P('grp', 'tp'), may hold values from -6 to 6
- parents: bfloat16 [128, 16, 2048], P('grp'), may hold values from -6 to 6
- parent_pairs: int32 [128, 2], P('grp'), may hold values from 0 to 127, as said below
- timestep: int32 [128], P('grp'), may hold values from 0 to 999
- valid_frames: int32 [128], P('grp'), may hold values from 4 to 16, as said below
- w_mod: bfloat16 [256, 6, 2048], P(None, None, 'tp'), may hold values from -0.375 to 0.375
- w_qkv: bfloat16 [2048, 3, 16, 128], P(None, None, 'tp'), may hold values from -0.125 to 0.125
- w_out: bfloat16 [16, 128, 2048], P('tp'), may hold values from -0.1875 to 0.1875
- w_cq: bfloat16 [2048, 16, 128], P(None, 'tp'), may hold values from -0.125 to 0.125
- w_ckv: bfloat16 [2048, 2, 16, 128], P(None, None, 'tp'), may hold values from -0.125 to 0.125
- w_cout: bfloat16 [16, 128, 2048], P('tp'), may hold values from -0.1875 to 0.1875
Outputs:
- next_frames: bfloat16 [32, 64, 16, 2048], P(None, 'grp', None, 'tp')
Inputs may be any that keep to these rules, and one draw needn't show every extreme that they name: `parent_pairs`: the first parent of group g is g - 1 or g, the second is g or g + 1, both kept within 0 to 127. Where g is a multiple of 4, the first parent is g - 1 (for g > 0); where g + 1 is a multiple of 4, the second is g + 1 (for g < 127). `valid_frames`: frames of a group at or past its count are padding and are never attended to.
All inputs are finite; a program needn't handle non-finite values.
Results may differ from a plain program's by a relative error of at most 0.019.
Values may be sent and summed in bfloat16 or wider, within the bound.
A program may use at most 128 MiB of HBM per device.

v0:
```python
import math

import jax
import jax.numpy as jnp
from jax import lax
from jax.sharding import PartitionSpec as P

D = 2048
HD = 128
TEMB = 256
F = 16
P_SIZE = 16


def with_halo(array, sides, width):
    for axis, dim in sides:
        size, length = (lax.axis_size(axis), array.shape[dim])
        up = [(i, (i + 1) % size) for i in range(size - 1)]
        down = [(j, i) for i, j in up]
        last = lax.slice_in_dim(array, length - width, length, axis=dim)
        leading = lax.slice_in_dim(array, 0, width, axis=dim)
        before = lax.ppermute(last, axis, up)
        after = lax.ppermute(leading, axis, down)
        array = jnp.concatenate([before, array, after], axis=dim)
    return array


def embed_time(stamp):
    half = TEMB // 2
    freq = jnp.exp(-math.log(10000.0) * jnp.arange(half, dtype=jnp.float32) / half)
    angle = stamp.astype(jnp.float32)[..., None] * freq
    return jax.nn.silu(jnp.concatenate([jnp.cos(angle), jnp.sin(angle)], axis=-1)).astype(
        jnp.bfloat16
    )


def layer_norm(values):
    centre = values - jnp.mean(values, axis=-1, keepdims=True)
    spread = jnp.mean(centre * centre, axis=-1, keepdims=True)
    return centre * lax.rsqrt(spread + 1e-06)


def attend(query, keys, vals, keep):
    scores = jnp.einsum(
        "gqhe,gkhe->ghqk", query, keys, preferred_element_type=jnp.float32
    ) / math.sqrt(HD)
    weights = jnp.exp(scores) * keep[:, None, None, :]
    probs = (weights / jnp.sum(weights, axis=-1, keepdims=True)).astype(jnp.bfloat16)
    return jnp.einsum("ghqk,gkhe->gqhe", probs, vals, preferred_element_type=jnp.float32).astype(
        jnp.bfloat16
    )


def on_device(
    latents, parents, parent_pairs, timestep, valid_frames, w_mod, w_qkv, w_out, w_cq, w_ckv, w_cout
):
    groups = parent_pairs.shape[0]
    rows = F * P_SIZE
    heads = w_qkv.shape[2]
    width = heads * HD
    local_feat = latents.shape[1]
    temb = embed_time(timestep)
    mod_local = jnp.einsum("gt,tkd->gkd", temb, w_mod, preferred_element_type=jnp.float32).astype(
        jnp.bfloat16
    )
    whole, mod_full = (
        lax.all_gather(latents, "tp", axis=1, tiled=True),
        lax.all_gather(mod_local, "tp", axis=2, tiled=True),
    )
    mod_full = mod_full.astype(jnp.float32)
    mod_part = mod_local.astype(jnp.float32)
    hidden = layer_norm(whole.astype(jnp.float32).reshape(groups, rows, D))
    hidden = (hidden * (1.0 + mod_full[:, 1:2]) + mod_full[:, 0:1]).astype(jnp.bfloat16)
    qkv = jnp.dot(
        hidden.reshape(groups * rows, D),
        w_qkv.reshape(D, 3 * width),
        preferred_element_type=jnp.float32,
    )
    qkv = qkv.astype(jnp.bfloat16).reshape(groups, rows, 3, heads, HD)
    frame = jnp.arange(rows, dtype=jnp.int32) // P_SIZE
    keep = (frame[None, :] < valid_frames[:, None]).astype(jnp.float32)
    attn = attend(qkv[:, :, 0], qkv[:, :, 1], qkv[:, :, 2], keep).reshape(groups * rows, width)
    partial_value = jnp.dot(attn, w_out.reshape(width, D), preferred_element_type=jnp.float32)
    branch = (
        lax.psum_scatter(partial_value.astype(jnp.bfloat16), "tp", scatter_dimension=1, tiled=True)
        .astype(jnp.float32)
        .reshape(groups, rows, local_feat)
    )
    own = latents.astype(jnp.float32).reshape(groups, rows, local_feat)
    x_local = (own + mod_part[:, 2:3] * branch).astype(jnp.bfloat16)
    x_full = lax.all_gather(
        x_local.reshape(groups * rows, local_feat), "tp", axis=1, tiled=True
    ).reshape(groups, rows, D)
    hidden2 = layer_norm(x_full.astype(jnp.float32))
    hidden2 = (hidden2 * (1.0 + mod_full[:, 4:5]) + mod_full[:, 3:4]).astype(jnp.bfloat16)
    cross_q = jnp.dot(
        hidden2.reshape(groups * rows, D),
        w_cq.reshape(D, width),
        preferred_element_type=jnp.float32,
    )
    cross_q = cross_q.astype(jnp.bfloat16).reshape(groups, rows, heads, HD)
    first_local = lax.axis_index("grp") * groups - 1
    chosen_index = (parent_pairs - first_local).reshape(-1)
    table = with_halo(parents, (("grp", 0),), 1)
    chosen = jnp.take(table, chosen_index, axis=0).reshape(groups * 2 * P_SIZE, D)
    cross_kv = jnp.dot(chosen, w_ckv.reshape(D, 2 * width), preferred_element_type=jnp.float32)
    cross_kv = cross_kv.astype(jnp.bfloat16).reshape(groups, 2 * P_SIZE, 2, heads, HD)
    ones = jnp.ones((groups, 2 * P_SIZE), jnp.float32)
    cattn = attend(cross_q, cross_kv[:, :, 0], cross_kv[:, :, 1], ones).reshape(
        groups * rows, width
    )
    partial2 = jnp.dot(cattn, w_cout.reshape(width, D), preferred_element_type=jnp.float32)
    branch2 = (
        lax.psum_scatter(partial2.astype(jnp.bfloat16), "tp", scatter_dimension=1, tiled=True)
        .astype(jnp.float32)
        .reshape(groups, rows, local_feat)
    )
    result = (x_local.astype(jnp.float32) + mod_part[:, 5:6] * branch2).astype(jnp.bfloat16)
    frames = groups * F
    result = result.reshape(frames, P_SIZE, local_feat)
    moved = lax.all_to_all(result, "grp", split_axis=0, concat_axis=0, tiled=True)
    sources = lax.axis_size("grp")
    return moved.reshape(sources, frames // sources, P_SIZE, local_feat)


def solution(mesh):
    in_specs = (
        P("grp", "tp"),
        P("grp", None, None),
        P("grp", None),
        P("grp"),
        P("grp"),
        P(None, None, "tp"),
        P(None, None, "tp", None),
        P("tp", None, None),
        P(None, "tp", None),
        P(None, None, "tp", None),
        P("tp", None, None),
    )
    out_specs = P(None, "grp", None, "tp")
    return jax.shard_map(
        on_device, mesh=mesh, in_specs=in_specs, out_specs=out_specs, check_vma=False
    )
```

profile of v0, /device:TPU:127, one launch (start us, length us, event | category | flops | bytes accessed | tf_op | source)
XLA Modules:
  0.0 541.8 jit_solution(17921853138577133456)
XLA Ops:
  6.5 0.7 all-gather.3.cloned.1.call-update
  7.3 0.7 convert_element_type.95
  8.1 1.3 fusion.44
  9.4 35.2 %all_gather.10 = bf16[4,6,2048]{2,0,1:T(4,128)(2,1)S(1)} all-gather(bf16[4,6,256]{2,0,1:T(4,128)(2,1)S(1)} %get-tuple-element.21), channel_id=1, replica_groups=mesh['grp'=32,'tp'=8] {'tp'}, dimensions={2}, use_global_device_ids=true | all-gather | bytes 110592 | tf_op jit(solution)/shard_map/all_gather | solution.py:68
  44.7 8.0 %reshape.227 = bf16[2048,768]{1,0:T(8,128)(2,1)} reshape(bf16[2048,3,2,128]{3,2,1,0:T(2,128)(2,1)} %param.17) | data formatting | bytes 6291456 | tf_op jit(solution)/shard_map/reshape | solution.py:76
  53.4 64.6 %all-gather.3.cloned.1.call-done = bf16[1024,2048]{1,0:T(8,128)(2,1)} async-done(((bf16[1024,256]{1,0:T(8,128)(2,1)}), bf16[1024,2048]{1,0:T(8,128)(2,1)}) %all-gather.3.cloned.1.call-update) | async-done | bytes 4194320 | tf_op jit(solution)/shard_map/all_gather | solution.py:67
  118.0 3.0 convert_reduce_fusion.1
  121.4 1.2 fusion.8
  122.7 1.9 fusion.11
  124.5 4.5 convolution_convert_fusion.2
  129.1 3.3 reshape.228
  132.4 2.3 fusion.41
  135.1 1.8 fusion.12
  138.0 3.2 convolution_convert_fusion.1
  141.5 122.7 %reduce-scatter.3.cloned.1.call-done = bf16[1024,256]{1,0:T(8,128)(2,1)} async-done(((bf16[1024,2048]{1,0:T(8,128)(2,1)}), bf16[1024,256]{1,0:T(8,128)(2,1)}) %reduce-scatter.3.cloned.1.call-update) | async-done | bytes 524304 | tf_op jit(solution)/shard_map/reduce_scatter | solution.py:85
  264.2 2.0 fusion.21
  266.3 4.6 collective-permute-start.1
  271.0 1.3 collective-permute-start
  272.6 2.7 reshape.234
  276.0 1.0 pad_maximum_fusion
  277.0 1.4 gather_fusion
  278.4 1.2 broadcast_select_fusion
  280.2 93.4 %all-gather.5.cloned.1.call-done = bf16[1024,2048]{1,0:T(8,128)(2,1)} async-done(((bf16[1024,256]{1,0:T(8,128)(2,1)}), bf16[1024,2048]{1,0:T(8,128)(2,1)}) %all-gather.5.cloned.1.call-update) | async-done | bytes 4194320 | tf_op jit(solution)/shard_map/all_gather | solution.py:91
  373.5 3.0 convert_reduce_fusion
  377.0 1.2 fusion.4
  378.2 1.9 fusion.7
  380.1 1.3 convolution_convert_fusion.5
  382.6 3.2 convolution_convert_fusion
  385.8 123.3 %reduce-scatter.5.cloned.1.call-done = bf16[1024,256]{1,0:T(8,128)(2,1)} async-done(((bf16[1024,2048]{1,0:T(8,128)(2,1)}), bf16[1024,256]{1,0:T(8,128)(2,1)}) %reduce-scatter.5.cloned.1.call-update) | async-done | bytes 524304 | tf_op jit(solution)/shard_map/reduce_scatter | solution.py:114
  509.2 1.4 fusion.19
  510.6 24.0 %all_to_all.5 = bf16[64,16,256]{2,1,0:T(8,128)(2,1)S(1)} all-to-all(bf16[64,16,256]{2,1,0:T(8,128)(2,1)S(1)} %fusion.19), channel_id=1, replica_groups=mesh['grp'=32,'tp'=8] {'grp'}, dimensions={0} | all-to-all | bytes 1048576 | tf_op jit(solution)/shard_map/all_to_all | solution.py:121
  534.5 0.8 copy.68
  (70 shorter events, 6.4 us)
Async XLA Ops:
  6.5 131.5 %copy-start = (bf16[2,128,2048]{2,1,0:T(8,128)(2,1)S(1)}, bf16[2,128,2048]{2,1,0:T(8,128)(2,1)}, u32[]{:S(2)}) copy-start(bf16[2,128,2048]{2,1,0:T(8,128)(2,1)} %param.18) | copy-start | bytes 3145732
  6.5 46.2 %copy-start.13 = (s32[4]{0:T(128)S(1)}, s32[4]{0:T(128)}, u32[]{:S(2)}) copy-start(s32[4]{0:T(128)} %param.15) | copy-start | bytes 52
  6.5 111.4 %all-gather.3.cloned.1.call-start = ((), (), s32[]{:S(2)}) async-start(), calls=%async_computation.3 | async-start | bytes 4718592 | tf_op jit(solution)/shard_map/all_gather | solution.py:67
  7.3 257.0 %reduce-scatter.3.cloned.1.call-start = ((), (), s32[]{:S(2)}) async-start(), calls=%async_computation.4 | async-start | bytes 4718592 | tf_op jit(solution)/shard_map/reduce_scatter | solution.py:85
  118.0 3.4 copy-start.2
  122.6 1.9 copy-start.5
  138.0 126.2 %copy-start.3 = (bf16[1024,256]{1,0:T(8,128)(2,1)S(1)}, bf16[1024,256]{1,0:T(8,128)(2,1)}, u32[]{:S(2)}) copy-start(bf16[1024,256]{1,0:T(8,128)(2,1)} %param.11) | copy-start | bytes 1572868
  141.2 125.1 %copy-start.8 = (bf16[4,16,2048]{2,1,0:T(8,128)(2,1)S(1)}, bf16[4,16,2048]{2,1,0:T(8,128)(2,1)}, u32[]{:S(2)}) copy-start(bf16[4,16,2048]{2,1,0:T(8,128)(2,1)} %param.12) | copy-start | bytes 786436
  141.2 131.1 %copy-start.12 = (s32[4,2]{0,1:T(2,128)S(1)}, s32[4,2]{0,1:T(2,128)}, u32[]{:S(2)}) copy-start(s32[4,2]{0,1:T(2,128)} %param.13) | copy-start | bytes 100
  141.2 232.3 %all-gather.5.cloned.1.call-start = ((), (), s32[]{:S(2)}) async-start(), calls=%async_computation.5 | async-start | bytes 4718592 | tf_op jit(solution)/shard_map/all_gather | solution.py:91
  266.2 242.9 %reduce-scatter.5.cloned.1.call-start = ((), (), s32[]{:S(2)}) async-start(), calls=%async_computation.6 | async-start | bytes 4718592 | tf_op jit(solution)/shard_map/reduce_scatter | solution.py:114
  266.3 9.0 %collective-permute-start.1 = (bf16[1,16,2048]{2,1,0:T(8,128)(2,1)S(1)}, bf16[1,16,2048]{2,1,0:T(8,128)(2,1)S(1)}, u32[]{:S(2)}, u32[]{:S(2)}) collective-permute-start(bf16[1,16,2048]{2,1,0:T(8,128)(2,1)S(1)} %get-tuple-element.9), channel_id=1, source_target_pairs={{8,0},{16,8},{24,16},{32,24},{40,32},{48,40},{56,48},{64,56},{72,6... | collective-permute-start | bytes 196616 | tf_op jit(solution)/shard_map/ppermute | solution.py:23
  271.0 5.0 collective-permute-start
  275.4 0.6 copy-start.11
  373.5 3.4 copy-start.1
  373.5 4.7 copy-start.9
  373.5 4.7 copy-start.10
  378.2 1.9 copy-start.14
  381.4 1.2 copy-start.7
  385.8 123.4 %copy-start.4 = (bf16[1024,256]{1,0:T(8,128)(2,1)S(1)}, bf16[1024,256]{1,0:T(8,128)(2,1)}, u32[]{:S(2)}) copy-start(bf16[1024,256]{1,0:T(8,128)(2,1)} %param.11) | copy-start | bytes 1572868
  385.8 123.4 %copy-start.6 = (bf16[1024,256]{1,0:T(8,128)(2,1)S(1)}, bf16[1024,256]{1,0:T(8,128)(2,1)}, u32[]{:S(2)}) copy-start(bf16[1024,256]{1,0:T(8,128)(2,1)} %reduce-scatter.3.cloned.1.call-done) | copy-start | bytes 1572868
Sparse Core Ops, SparseCore 0:
  9.8 108.0 all-gather.2
  141.4 122.8 reduce-scatter.2
  266.7 106.7 all-gather.4
  386.0 123.1 reduce-scatter.4
where the time goes:
time: 548 us; the launch traced here: 542 us
  waiting for transfers between devices  405 us (74%)
  blocking collectives  59.2 us (11%)
  local copies, waits for them, and re-layouts  22 us (4%)
  other arithmetic  19.2 us (4%)
  matrix products  17.1 us (3%)
  between operations  13.5 us (2%)
  starting transfers between devices  6.22 us (1%)
    reduce_scatter x1, waiting for transfers between devices, on_device(): lax.psum_scatter(partial2.astype(jnp.bfloat16), 'tp', scatter_dimension=1...  123 us
    reduce_scatter x1, waiting for transfers between devices, on_device(): lax.psum_scatter(partial_value.astype(jnp.bfloat16), 'tp', scatter_dimens...  123 us
    all_gather x1, waiting for transfers between devices, on_device(): lax.all_gather(x_local.reshape(groups * rows, local_feat), 'tp', axis=1,...  93.4 us
    all_gather x1, waiting for transfers between devices, on_device(): lax.all_gather(latents, 'tp', axis=1, tiled=True)  64.6 us
    all_gather x1, blocking collectives, on_device(): lax.all_gather(mod_local, 'tp', axis=2, tiled=True)  35.2 us
    all_to_all x1, blocking collectives, on_device(): lax.all_to_all(result, 'grp', split_axis=0, concat_axis=0, tiled=True)  24 us
  transfers between devices with their start and end apart: 6, of which 4 were waited for; matrix products, arithmetic and copies ran while one was open for 3% of the time, Pallas kernels for 0%

commit v1 on v0

v1 whole, which is shorter than its diff:
```python
import math

import jax
import jax.numpy as jnp
from jax import lax
from jax.experimental import pallas as pl
from jax.experimental.pallas import tpu as pltpu
from jax.sharding import PartitionSpec as P

D = 2048
HD = 128
TEMB = 256
F = 16
P_SIZE = 16
ROWS = F * P_SIZE
EXT = ROWS + 16
MESH = pl.DeviceIdType.MESH
BF = jnp.bfloat16
F32 = jnp.float32
QUERY, CROSS, OUT, COUT = range(4)
WEIGHT_ROWS = (D, D, 2 * HD, 2 * HD)


def embed_time(stamp):
    half = TEMB // 2
    freq = jnp.exp(-math.log(10000.0) * jnp.arange(half, dtype=jnp.float32) / half)
    angle = stamp.astype(jnp.float32)[..., None] * freq
    return jax.nn.silu(jnp.concatenate([jnp.cos(angle), jnp.sin(angle)], axis=-1)).astype(BF)


def norm_rows(values, scale, shift):
    centre = values - jnp.mean(values, axis=-1, keepdims=True)
    spread = jnp.mean(centre * centre, axis=-1, keepdims=True)
    return centre * lax.rsqrt(spread + 1e-06) * (1.0 + scale) + shift


def kernel(
    lat, modx, parents, wqkv, wckv, wcq, wout, wcout, pairs, out,
    rows_all, z_source, w_query, w_cross, w_out, w_cout, table, chosen, hidden, qkv, attn,
    branch_send, branch_recv, fold_send, fold, x_one, result, blocks,
    local_sem, send_sem, recv_sem, final_sem, out_sem,
):
    grp, tp = lax.axis_index("grp"), lax.axis_index("tp")
    c, y, zlo = lax.rem(grp, 2), lax.rem(lax.div(grp, 2), 4), lax.div(grp, 8)
    x, zhi = lax.div(tp, 2), lax.rem(tp, 2)
    z = zhi * 4 + zlo
    other = 1 - zhi
    step_z = 1 - 2 * c
    place = c * 3 + step_z * zlo
    is_source = lax.div(place, 3)

    def dev(dx=0, dy=0, dz=0, dc=0):
        xx, yy = lax.rem(x + dx + 4, 4), lax.rem(y + dy + 4, 4)
        zz, cc = lax.rem(z + dz + 8, 8), lax.rem(c + dc, 2)
        return {
            "grp": (lax.rem(zz, 4) * 4 + yy) * 2 + cc,
            "tp": xx * 2 + lax.div(zz, 4),
        }

    names = {}

    def sem_id(*name):
        return names.setdefault(name, len(names))

    sends = []

    def remote(src, dst, name, target, extra=0, note=True):
        copy = pltpu.make_async_remote_copy(
            src_ref=src, dst_ref=dst, send_sem=send_sem.at[sem_id(*name)],
            recv_sem=recv_sem.at[sem_id(*name) + extra], device_id=target, device_id_type=MESH,
        )
        if note:
            sends.append(copy)
        return copy

    def arrived(region, name, extra=0):
        pltpu.make_async_remote_copy(
            src_ref=region, dst_ref=region, send_sem=send_sem.at[0],
            recv_sem=recv_sem.at[sem_id(*name) + extra], device_id=dev(dc=1), device_id_type=MESH,
        ).wait_recv()

    locals_used = [0]

    def local(src, dst):
        copy = pltpu.make_async_copy(src, dst, local_sem.at[locals_used[0]])
        locals_used[0] += 1
        copy.start()
        return copy

    def columns(index):
        return pl.ds(pl.multiple_of(index * 256, 256), 256)

    load_z = [
        local(lat.at[pl.ds(2 * other, 2)], z_source.at[:, 0:ROWS, :]),
        local(modx.at[pl.ds(2 * other, 2)], z_source.at[:, ROWS:EXT, :]),
    ]
    load_own = [
        local(lat.at[pl.ds(2 * zhi, 2)], rows_all.at[:, 0:ROWS, columns(tp)]),
        local(modx.at[pl.ds(2 * zhi, 2)], rows_all.at[:, ROWS:EXT, columns(tp)]),
    ]
    load_query = [
        local(wqkv.at[i], w_query.at[zhi, :, i * HD : (i + 1) * HD]) for i in range(6)
    ]
    load_cross = [
        local(wckv.at[i], w_cross.at[zhi, :, i * HD : (i + 1) * HD]) for i in range(4)
    ] + [
        local(wcq.at[i], w_cross.at[zhi, :, (4 + i) * HD : (5 + i) * HD]) for i in range(2)
    ]
    load_out = [local(wout, w_out.at[zhi])]
    load_cout = [local(wcout, w_cout.at[zhi])]
    load_table = [local(parents.at[pl.ds(zhi, 3)], table.at[pl.ds(other, 3)])]

    barrier = pltpu.get_barrier_semaphore()

    def greet(target):
        pl.semaphore_signal(barrier, inc=1, device_id=target, device_id_type=MESH)

    greet(dev(dx=1))
    greet(dev(dx=-1))
    greet(dev(dx=2))
    greet(dev(dz=4))
    greet(dev(dz=-step_z))
    greet(dev(dy=1))
    greet(dev(dy=-1))
    greet(dev(dc=1))
    greet({"grp": lax.rem(grp + 2 * zhi - 1 + 32, 32), "tp": tp})
    owner = lax.div(x, 2) == c
    own_group = lax.rem(x, 2)

    @pl.loop(0, 32)
    def _(i):
        source_c = lax.rem(i, 2)
        source_tp = (2 * source_c + lax.rem(zlo, 2)) * 2 + lax.div(zlo, 2)

        @pl.when(jnp.logical_or(i != grp, source_tp != tp))
        def _():
            greet({"grp": i, "tp": source_tp})

    to_self = (zlo == 2 * zhi + own_group).astype(jnp.int32)
    pl.semaphore_wait(barrier, 9 + owner.astype(jnp.int32) * (64 - to_self))

    def slab(group, tp_index):
        return rows_all.at[group, :, columns(tp_index)]

    for copy in load_z:
        copy.wait()
    for group in range(2):
        remote(z_source.at[group], slab(group, tp), ("z", group), dev(dz=4)).start()
    for copy in load_own:
        copy.wait()

    def spread(kind, tp_index):
        for group in range(2):
            for way in (1, -1):
                ref = slab(group, tp_index)
                remote(ref, ref, ("x", kind, group, way), dev(dx=way)).start()

    def tp_at(dx, kind):
        return lax.rem(x + dx + 4, 4) * 2 + (zhi if kind == 0 else other)

    def spread_relay(kind):
        for group, way in ((0, 1), (1, -1)):
            ref = slab(group, tp_at(-way, kind))
            arrived(ref, ("x", kind, group, way))
            remote(ref, ref, ("xr", kind, group), dev(dx=way)).start()

    def spread_end(kind):
        for group, way in ((0, -1), (1, 1)):
            arrived(slab(group, tp_at(-way, kind)), ("x", kind, group, way))
        for group in range(2):
            arrived(slab(group, tp_at(2, kind)), ("xr", kind, group))

    spread(0, tp)
    remote(
        parents.at[3 * other], table.at[3 * zhi], ("halo",),
        {"grp": lax.rem(grp + 1 - 2 * zhi + 32, 32), "tp": tp},
    ).start()

    buffers = (w_query, w_cross, w_out, w_cout)
    slice_sent = is_source * zhi + (1 - is_source) * other

    def part(which, index, quarter, core, sub=None):
        rows = WEIGHT_ROWS[which]
        start = quarter * (rows // 4) + core * (rows // 8)
        size = rows // 8
        if sub is not None:
            size = rows // 16
            start = start + sub * size
        return buffers[which].at[index, pl.ds(pl.multiple_of(start, rows // 16), size), :]

    chain_copies = {}

    def chain_prepare(which):
        for sub in range(2):
            ref = part(which, slice_sent, y, c, sub)
            chain_copies[which, sub] = remote(ref, ref, ("chain", which, sub), dev(dz=step_z))

    def chain_start(which):
        chain_prepare(which)

        @pl.when(is_source == 1)
        def _():
            for sub in range(2):
                chain_copies[which, sub].start()

    def chain_relay(which):
        for sub in range(2):
            ref = part(which, other, y, c, sub)
            arrived(ref, ("chain", which, sub))

            @pl.when(is_source == 0)
            def _():
                chain_copies[which, sub].start()

            for way in (1, -1):
                remote(ref, ref, ("y", which, sub, way), dev(dy=way)).start()

    def quarter_at(dy):
        return lax.rem(y + dy + 4, 4)

    def core_forward(which, dy):
        ref = part(which, other, quarter_at(dy), c)
        remote(ref, ref, ("core", which, dy), dev(dc=1)).start()

    def y_relay(which):
        for sub, way in ((0, 1), (1, -1)):
            ref = part(which, other, quarter_at(-way), c, sub)
            arrived(ref, ("y", which, sub, way))
            remote(ref, ref, ("yr", which, sub), dev(dy=way)).start()
        core_forward(which, 0)

    def y_end(which):
        for sub, way in ((1, 1), (0, -1)):
            arrived(part(which, other, quarter_at(-way), c, sub), ("y", which, sub, way))
            core_forward(which, -way)
        for sub in range(2):
            arrived(part(which, other, quarter_at(2), c, sub), ("yr", which, sub))
        core_forward(which, 2)
        for dy in (0, 1, -1, 2):
            arrived(part(which, other, quarter_at(dy), 1 - c), ("core", which, dy))

    for copy in load_query:
        copy.wait()
    chain_start(QUERY)

    def choose():
        for copy in load_table:
            copy.wait()
        arrived(table.at[3 * zhi], ("halo",))
        for group in range(2):
            index = grp * 4 + 2 * zhi + group
            first = pairs[2 * zhi + group, 0]
            second = pairs[2 * zhi + group, 1]
            chosen[group * 32 : group * 32 + 16, :] = jnp.where(
                first == index - 1, table[group], table[group + 1]
            )
            chosen[group * 32 + 16 : group * 32 + 32, :] = jnp.where(
                second == index + 1, table[group + 2], table[group + 1]
            )

    def fold_slice(phase, index):
        kv = jnp.dot(chosen[...], w_cross[index, :, 0:512], preferred_element_type=F32).astype(BF)
        for head in range(2):
            key = kv[:, head * HD : (head + 1) * HD]
            value = kv[:, 256 + head * HD : 256 + (head + 1) * HD]
            for n in range(4):
                cols = slice(n * 512, (n + 1) * 512)
                left = lax.dot_general(
                    key, w_cross[index, cols, 512 + head * HD : 512 + (head + 1) * HD],
                    (((1,), (1,)), ((), ())), preferred_element_type=F32,
                ) * (1.0 / math.sqrt(HD))
                right = jnp.dot(
                    value, w_cout[index, head * HD : (head + 1) * HD, cols],
                    preferred_element_type=F32,
                )
                for group in range(2):
                    there = slice(head * 32, head * 32 + 32)
                    here = slice(group * 32, group * 32 + 32)
                    fold_send[0, group, phase, there, cols] = left[here].astype(BF)
                    fold_send[1, group, phase, there, cols] = right[here].astype(BF)

    def fold_start(phase):
        index = zhi if phase == 0 else other
        base = sem_id("fold", phase, 0)
        for extra in range(1, 8):
            sem_id("fold", phase, extra)
        del base
        for group in range(2):
            for side in range(2):
                rows = pl.ds(pl.multiple_of(x * 128 + index * 64, 64), 64)
                src, dst = fold_send.at[side, group, phase], fold.at[side, rows, :]
                copy = pltpu.make_async_remote_copy(
                    src_ref=src, dst_ref=dst, send_sem=send_sem.at[sem_id("fs", phase, group, side)],
                    recv_sem=recv_sem.at[sem_id("fold", phase, 0) + x * 2 + side],
                    device_id={"grp": grp, "tp": (2 * c + group) * 2 + zhi}, device_id_type=MESH,
                )

                @pl.when(x == 2 * c + group)
                def _():
                    pltpu.make_async_copy(
                        src, dst, recv_sem.at[sem_id("fold", phase, 0) + x * 2 + side]
                    ).start()

                @pl.when(x != 2 * c + group)
                def _():
                    copy.start()

                guarded.append((x != 2 * c + group, copy))

    guarded = []

    def normalise(group):
        mod = rows_all[group, ROWS:EXT, :].astype(F32)
        shift, scale = mod[0:1], mod[1:2]

        @pl.loop(0, ROWS // 32)
        def _(i):
            rows = pl.ds(pl.multiple_of(i * 32, 32), 32)
            values = rows_all[group, rows, :].astype(F32)
            hidden[group, rows, :] = norm_rows(values, scale, shift).astype(BF)

    def attend(group):
        mod = rows_all[group, ROWS:EXT, 0:256].astype(F32)
        frame = lax.div(lax.broadcasted_iota(jnp.int32, (1, ROWS), 1), P_SIZE).astype(F32)
        keep = (frame < mod[6:7]).astype(F32)

        @pl.loop(0, 2)
        def _(s):
            for n in range(3):
                cols = slice(n * 256, (n + 1) * 256)
                qkv[:, cols] = jnp.dot(
                    hidden[group], w_query[s, :, cols], preferred_element_type=F32
                ).astype(BF)
            for head in range(2):
                cols = slice(head * HD, (head + 1) * HD)
                query = qkv[:, cols]
                key = qkv[:, 256 + head * HD : 256 + (head + 1) * HD]
                value = qkv[:, 512 + head * HD : 512 + (head + 1) * HD]
                scores = lax.dot_general(
                    query, key, (((1,), (1,)), ((), ())), preferred_element_type=F32
                ) * (1.0 / math.sqrt(HD))
                weights = jnp.exp(scores) * keep
                probs = (weights / jnp.sum(weights, axis=-1, keepdims=True)).astype(BF)
                attn[s, :, cols] = jnp.dot(probs, value, preferred_element_type=F32).astype(BF)

    def project(group):
        for n in range(4):
            cols = slice(n * 512, (n + 1) * 512)
            total = jnp.dot(attn[0], w_out[0, :, cols], preferred_element_type=F32)
            total = total + jnp.dot(attn[1], w_out[1, :, cols], preferred_element_type=F32)
            branch_send[group, :, cols] = total.astype(BF)
        src, dst = branch_send.at[group], branch_recv.at[x]
        base = sem_id("branch", 0)
        for index in range(1, 4):
            sem_id("branch", index)
        copy = pltpu.make_async_remote_copy(
            src_ref=src, dst_ref=dst, send_sem=send_sem.at[sem_id("bs", group)],
            recv_sem=recv_sem.at[base + x],
            device_id={"grp": grp, "tp": (2 * c + group) * 2 + zhi}, device_id_type=MESH,
        )

        @pl.when(x == 2 * c + group)
        def _():
            pltpu.make_async_copy(src, dst, recv_sem.at[base + x]).start()

        @pl.when(x != 2 * c + group)
        def _():
            copy.start()

        guarded.append((x != 2 * c + group, copy))

    spread_relay(0)
    chain_relay(QUERY)
    for group in range(2):
        arrived(slab(group, tp_at(0, 1)), ("z", group))
    spread(1, tp_at(0, 1))
    for copy in load_out + load_cross + load_cout:
        copy.wait()
    chain_start(OUT)
    chain_start(CROSS)
    chain_start(COUT)
    blocks[...] = (
        lax.div(lax.broadcasted_iota(jnp.int32, (512, 512), 0), 32)
        == lax.div(lax.broadcasted_iota(jnp.int32, (512, 512), 1), 32)
    ).astype(F32).astype(BF)
    choose()
    fold_slice(0, zhi)
    spread_relay(1)
    y_relay(QUERY)
    spread_end(0)
    spread_end(1)
    fold_start(0)
    normalise(0)
    chain_relay(OUT)
    normalise(1)
    y_end(QUERY)
    y_relay(OUT)
    attend(0)
    y_end(OUT)
    chain_relay(CROSS)
    project(0)
    attend(1)
    project(1)
    y_relay(CROSS)
    chain_relay(COUT)
    y_end(CROSS)
    y_relay(COUT)
    y_end(COUT)
    fold_slice(1, other)
    fold_start(1)

    def final_copy(i):
        near, far = lax.div(i, 8), lax.rem(i, 8)
        target = (2 * zhi + own_group) * 8 + near
        src = result.at[pl.ds(pl.multiple_of(near * 32, 32), 32), columns(far)]
        dst = out.at[grp]
        return target, far, src, dst, pltpu.make_async_remote_copy(
            src_ref=src, dst_ref=dst, send_sem=final_sem.at[i], recv_sem=out_sem,
            device_id={"grp": target, "tp": far}, device_id_type=MESH,
        )

    @pl.when(owner)
    def _():
        for index in range(4):
            arrived(branch_recv.at[index], ("branch", 0), index)
        mod = rows_all[own_group, ROWS:EXT, :].astype(F32)
        gate1, shift2, scale2, gate2 = mod[2:3], mod[3:4], mod[4:5], mod[5:6]

        @pl.loop(0, ROWS // 32)
        def _(i):
            rows = pl.ds(pl.multiple_of(i * 32, 32), 32)
            total = branch_recv[0, rows, :].astype(F32)
            for index in range(1, 4):
                total = total + branch_recv[index, rows, :].astype(F32)
            value = (rows_all[own_group, rows, :].astype(F32) + gate1 * total).astype(BF)
            x_one[rows, :] = value
            hidden[0, rows, :] = norm_rows(value.astype(F32), scale2, shift2).astype(BF)

        for phase in range(2):
            index = zhi if phase == 0 else other
            for source in range(4):
                rows = pl.ds(pl.multiple_of(source * 128 + index * 64, 64), 64)
                for side in range(2):
                    arrived(fold.at[side, rows, :], ("fold", phase, 0), source * 2 + side)

        @pl.loop(0, 2)
        def _(i):
            rows = pl.ds(pl.multiple_of(i * 128, 128), 128)
            scores = lax.dot_general(
                hidden[0, rows, :], fold[0], (((1,), (1,)), ((), ())), preferred_element_type=F32
            )
            weights = jnp.exp(scores).astype(BF)
            total = jnp.dot(weights, blocks[...], preferred_element_type=F32)
            probs = (weights.astype(F32) / total).astype(BF)
            for n in range(4):
                cols = slice(n * 512, (n + 1) * 512)
                branch = jnp.dot(probs, fold[1, :, cols], preferred_element_type=F32)
                result[rows, cols] = (
                    x_one[rows, cols].astype(F32) + gate2[:, cols] * branch
                ).astype(BF)

            @pl.loop(i * 32, i * 32 + 32)
            def _(j):
                target, far, src, dst, copy = final_copy(j)
                mine = jnp.logical_and(target == grp, far == tp)

                @pl.when(mine)
                def _():
                    pltpu.make_async_copy(src, dst, out_sem).start()

                @pl.when(jnp.logical_not(mine))
                def _():
                    copy.start()

    for copy in sends:
        copy.wait_send()
    for condition, copy in guarded:

        @pl.when(condition)
        def _():
            copy.wait_send()

    @pl.when(owner)
    def _():
        @pl.loop(0, 64)
        def _(j):
            target, far, src, dst, copy = final_copy(j)

            @pl.when(jnp.logical_or(target != grp, far != tp))
            def _():
                copy.wait_send()

    pltpu.make_async_remote_copy(
        src_ref=out, dst_ref=out, send_sem=send_sem.at[0], recv_sem=out_sem,
        device_id=dev(dc=1), device_id_type=MESH,
    ).wait_recv()
    assert len(names) <= 192 and locals_used[0] <= 32


def on_device(
    latents, parents, parent_pairs, timestep, valid_frames, w_mod, w_qkv, w_out, w_cq, w_ckv, w_cout
):
    groups = parent_pairs.shape[0]
    temb = embed_time(timestep)
    mod = jnp.einsum("gt,tkd->gkd", temb, w_mod, preferred_element_type=F32).astype(BF)
    valid = jnp.broadcast_to(valid_frames.astype(BF)[:, None, None], (groups, 1, 256))
    modx = jnp.concatenate([mod, valid, jnp.zeros((groups, 9, 256), BF)], axis=1)
    wqkv = w_qkv.transpose(1, 2, 0, 3).reshape(6, D, HD)
    wckv = w_ckv.transpose(1, 2, 0, 3).reshape(4, D, HD)
    wcq = w_cq.transpose(1, 0, 2)
    hbm = pl.BlockSpec(memory_space=pl.ANY)
    moved = pl.pallas_call(
        kernel,
        out_shape=jax.ShapeDtypeStruct((32, 32, 256), BF),
        in_specs=[hbm] * 8 + [pl.BlockSpec(memory_space=pltpu.SMEM)],
        out_specs=hbm,
        scratch_shapes=[
            pltpu.VMEM((2, EXT, D), BF),
            pltpu.VMEM((2, EXT, 256), BF),
            pltpu.VMEM((2, D, 768), BF),
            pltpu.VMEM((2, D, 768), BF),
            pltpu.VMEM((2, 2 * HD, D), BF),
            pltpu.VMEM((2, 2 * HD, D), BF),
            pltpu.VMEM((4, P_SIZE, D), BF),
            pltpu.VMEM((64, D), BF),
            pltpu.VMEM((2, ROWS, D), BF),
            pltpu.VMEM((ROWS, 768), BF),
            pltpu.VMEM((2, ROWS, 2 * HD), BF),
            pltpu.VMEM((2, ROWS, D), BF),
            pltpu.VMEM((4, ROWS, D), BF),
            pltpu.VMEM((2, 2, 2, 64, D), BF),
            pltpu.VMEM((2, 512, D), BF),
            pltpu.VMEM((ROWS, D), BF),
            pltpu.VMEM((ROWS, D), BF),
            pltpu.VMEM((512, 512), BF),
            pltpu.SemaphoreType.DMA((32,)),
            pltpu.SemaphoreType.DMA((192,)),
            pltpu.SemaphoreType.DMA((192,)),
            pltpu.SemaphoreType.DMA((64,)),
            pltpu.SemaphoreType.DMA,
        ],
        compiler_params=pltpu.CompilerParams(
            collective_id=0, has_side_effects=True, vmem_limit_bytes=58 << 20
        ),
        name="dit_block",
    )(
        latents.reshape(groups, ROWS, 256), modx, parents, wqkv, wckv, wcq,
        w_out.reshape(2 * HD, D), w_cout.reshape(2 * HD, D), parent_pairs,
    )
    return moved.reshape(32, 2, P_SIZE, 256)


def solution(mesh):
    in_specs = (
        P("grp", "tp"),
        P("grp", None, None),
        P("grp", None),
        P("grp"),
        P("grp"),
        P(None, None, "tp"),
        P(None, None, "tp", None),
        P("tp", None, None),
        P(None, "tp", None),
        P(None, None, "tp", None),
        P("tp", None, None),
    )
    out_specs = P(None, "grp", None, "tp")
    return jax.shard_map(
        on_device, mesh=mesh, in_specs=in_specs, out_specs=out_specs, check_vma=False
    )
```

time: 548 us -> 155 us (0.28); the launches traced: 542 us -> 155 us
  waiting for transfers between devices: 405 us -> 0 us
  Pallas kernels: 0 us -> 143 us
  blocking collectives: 59.2 us -> 0 us
  matrix products: 17.1 us -> 0.22 us
  other arithmetic: 19.2 us -> 2.35 us
  between operations: 13.5 us -> 0.02 us
  local copies, waits for them, and re-layouts: 22 us -> 9.56 us
  starting transfers between devices: 6.22 us -> 0 us
    reduce_scatter x2 -> x0, waiting for transfers between devices: 246 us -> none  [the longest x1 123 us: on_device(): lax.psum_scatter(partial2.astype(jnp.bfloat16), 'tp', scatter_dimension=1...]
    all_gather x2 -> x0, waiting for transfers between devices: 158 us -> none  [the longest x1 93.4 us: on_device(): lax.all_gather(x_local.reshape(groups * rows, local_feat), 'tp', axis=1,...]
    pallas_call x0 -> x1, Pallas kernels: none -> 143 us  [on_device(): pl.pallas_call(kernel, out_shape=jax.ShapeDtypeStruct((32, 32, 256), BF),...]
    all_gather x1 -> x0, blocking collectives: 35.2 us -> none  [on_device(): lax.all_gather(mod_local, 'tp', axis=2, tiled=True)]
    all_to_all x1 -> x0, blocking collectives: 24 us -> none  [on_device(): lax.all_to_all(result, 'grp', split_axis=0, concat_axis=0, tiled=True)]
    dot_general x10 -> x1, matrix products: 17.1 us -> 0.22 us  [on_device(): jnp.einsum('gt,tkd->gkd', temb, w_mod, preferred_element_type=F32)]
    reshape x7 -> x0, local copies, waits for them, and re-layouts: 14.4 us -> none  [the longest x1 8.03 us: on_device(): w_qkv.reshape(D, 3 * width)]
    reduce_sum x4 -> x0, other arithmetic: 8.35 us -> none  [the longest x2 5.9 us: layer_norm(): centre = values - jnp.mean(values, axis=-1, keepdims=True)]
  transfers between devices with their start and end apart: 6 -> 0, of which waited for: 4 -> 0; matrix products, arithmetic and copies ran while one was open for 3% -> 0% of each run, Pallas kernels for 0% -> 0%
where the time goes in v1:
time: 155 us
  Pallas kernels  143 us (92%)
  local copies, waits for them, and re-layouts  9.56 us (6%)
  other arithmetic  2.35 us (2%)
    pallas_call x1, Pallas kernels, on_device(): pl.pallas_call(kernel, out_shape=jax.ShapeDtypeStruct((32, 32, 256), BF),...  143 us
    unnamed x9, local copies, waits for them, and re-layouts  5.72 us

profile of v1, /device:TPU:127, one launch (start us, length us, event | category | flops | bytes accessed | tf_op | source)
XLA Modules:
  0.0 155.1 jit_solution(7517672598049293759)
XLA Ops:
  0.0 0.0 copy-start
  0.0 0.0 copy-start.2
  0.0 0.8 convert_element_type.12
  0.8 0.7 convert_element_type.15
  1.5 0.1 pad.2.clone
  1.6 1.3 copy.21.pairs
  3.0 0.1 multiply_cosine_fusion
  3.1 0.1 broadcast_in_dim.4
  3.2 0.0 copy-done
  3.2 0.2 convolution_convert_fusion
  3.4 0.7 maximum_maximum_fusion.modx
  4.1 0.0 copy-start.1
  4.1 2.5 %copy.23 = bf16[2048,2,128]{2,0,1:T(8,128)(2,1)} copy(bf16[2048,2,128]{2,1,0:T(2,128)(2,1)} %param.19) | data formatting | bytes 2097152 | tf_op args[8]
  6.6 0.0 copy-done.2
  6.6 1.6 %copy.19 = bf16[2,2,2048,128]{3,2,1,0:T(8,128)(2,1)} copy(bf16[2,2,2048,128]{3,1,0,2:T(2,128)(2,1)S(1)} %bitcast.19) | data formatting | bytes 4194304 | tf_op jit(solution)/shard_map/transpose | solution.py:509
  8.2 0.0 copy-done.1
  8.2 2.1 %copy.18 = bf16[3,2,2048,128]{3,2,1,0:T(8,128)(2,1)} copy(bf16[3,2,2048,128]{3,1,0,2:T(2,128)(2,1)S(1)} %bitcast.18) | data formatting | bytes 6291456 | tf_op jit(solution)/shard_map/transpose | solution.py:508
  10.3 143.0 %dit_block.1 = bf16[32,32,256]{2,1,0:T(8,128)(2,1)} custom-call(bf16[4,256,256]{2,1,0:T(8,128)(2,1)} %bitcast.23, bf16[4,16,256]{2,1,0:T(8,128)(2,1)} %maximum_maximum_fusion.modx, bf16[4,16,2048]{2,1,0:T(8,128)(2,1)} %parents.1, bf16[6,2048,128]{2,1,0:T(8,128)(2,1)} %bitcast.15, bf16[4,2048,128]{2,1,0:T(8,128)(2,1)} %bitcast.16, ...), custom_call_target="tpu_custom_call" | custom-call | tf_op jit(solution)/shard_map/dit_block/pallas_call | solution.py:512
  153.2 1.9 %copy.25 = bf16[32,2,16,256]{3,2,1,0:T(8,128)(2,1)} copy(bf16[32,2,16,256]{3,2,1,0:T(8,128)(2,1)} %bitcast.20) | data formatting | bytes 1048576
  (3 shorter events, 0.0 us)
Async XLA Ops:
  0.0 3.2 %copy-start = (bf16[256,6,256]{2,0,1:T(8,128)(2,1)S(1)}, bf16[256,6,256]{2,0,1:T(8,128)(2,1)}, u32[]{:S(2)}) copy-start(bf16[256,6,256]{2,0,1:T(8,128)(2,1)} %param.16) | copy-start | bytes 2359300
  0.0 6.6 %copy-start.2 = (bf16[2048,2,2,128]{3,2,1,0:T(2,128)(2,1)S(1)}, bf16[2048,2,2,128]{3,2,1,0:T(2,128)(2,1)}, u32[]{:S(2)}) copy-start(bf16[2048,2,2,128]{3,2,1,0:T(2,128)(2,1)} %param.20) | copy-start | bytes 6291460
  4.1 4.1 %copy-start.1 = (bf16[2048,3,2,128]{3,2,1,0:T(2,128)(2,1)S(1)}, bf16[2048,3,2,128]{3,2,1,0:T(2,128)(2,1)}, u32[]{:S(2)}) copy-start(bf16[2048,3,2,128]{3,2,1,0:T(2,128)(2,1)} %param.17) | copy-start | bytes 9437188

commit v2 on v1

--- a/solution.py
+++ b/solution.py
@@ -17,8 +17,8 @@
 MESH = pl.DeviceIdType.MESH
 BF = jnp.bfloat16
 F32 = jnp.float32
-QUERY, CROSS, OUT, COUT = range(4)
-WEIGHT_ROWS = (D, D, 2 * HD, 2 * HD)
+KEYS, VALUES, CROSS, OUT, COUT = range(5)
+WEIGHT_ROWS = (D, D, D, 2 * HD, 2 * HD)
 
 
 def embed_time(stamp):
@@ -36,7 +36,7 @@
 
 def kernel(
     lat, modx, parents, wqkv, wckv, wcq, wout, wcout, pairs, out,
-    rows_all, z_source, w_query, w_cross, w_out, w_cout, table, chosen, hidden, qkv, attn,
+    rows_all, z_source, w_query, w_cross, w_out, w_cout, w_kv, table, chosen, kv_own, kv_other, hidden, qkv, attn,
     branch_send, branch_recv, fold_send, fold, x_one, result, blocks,
     local_sem, send_sem, recv_sem, final_sem, out_sem,
 ):
@@ -49,6 +49,9 @@
     place = c * 3 + step_z * zlo
     is_source = lax.div(place, 3)
 
+    def group_at(half, index):
+        return (1 - half) * 3 * index + half * (1 + index)
+
     def dev(dx=0, dy=0, dz=0, dc=0):
         xx, yy = lax.rem(x + dx + 4, 4), lax.rem(y + dy + 4, 4)
         zz, cc = lax.rem(z + dz + 8, 8), lax.rem(c + dc, 2)
@@ -90,27 +93,28 @@
     def columns(index):
         return pl.ds(pl.multiple_of(index * 256, 256), 256)
 
-    load_z = [
-        local(lat.at[pl.ds(2 * other, 2)], z_source.at[:, 0:ROWS, :]),
-        local(modx.at[pl.ds(2 * other, 2)], z_source.at[:, ROWS:EXT, :]),
-    ]
-    load_own = [
-        local(lat.at[pl.ds(2 * zhi, 2)], rows_all.at[:, 0:ROWS, columns(tp)]),
-        local(modx.at[pl.ds(2 * zhi, 2)], rows_all.at[:, ROWS:EXT, columns(tp)]),
-    ]
+    load_z, load_own = [], []
+    for group in range(2):
+        there, here = group_at(other, group), group_at(zhi, group)
+        load_z.append(local(lat.at[there], z_source.at[group, 0:ROWS, :]))
+        load_z.append(local(modx.at[there], z_source.at[group, ROWS:EXT, :]))
+        load_own.append(local(lat.at[here], rows_all.at[group, 0:ROWS, columns(tp)]))
+        load_own.append(local(modx.at[here], rows_all.at[group, ROWS:EXT, columns(tp)]))
     load_query = [
         local(wqkv.at[i], w_query.at[zhi, :, i * HD : (i + 1) * HD]) for i in range(6)
     ]
     load_cross = [
-        local(wckv.at[i], w_cross.at[zhi, :, i * HD : (i + 1) * HD]) for i in range(4)
-    ] + [
-        local(wcq.at[i], w_cross.at[zhi, :, (4 + i) * HD : (5 + i) * HD]) for i in range(2)
+        local(wcq.at[i], w_cross.at[zhi, :, i * HD : (i + 1) * HD]) for i in range(2)
     ]
+    load_cout = [local(wcout, w_cout.at[zhi])]
     load_out = [local(wout, w_out.at[zhi])]
-    load_cout = [local(wcout, w_cout.at[zhi])]
-    load_table = [local(parents.at[pl.ds(zhi, 3)], table.at[pl.ds(other, 3)])]
+    load_kv = [local(wckv.at[i], w_kv.at[:, i * HD : (i + 1) * HD]) for i in range(4)]
+    load_table = [local(parents, table.at[1:5])]
 
     barrier = pltpu.get_barrier_semaphore()
+
+    def grp_at(step):
+        return {"grp": lax.rem(grp + step + 32, 32), "tp": tp}
 
     def greet(target):
         pl.semaphore_signal(barrier, inc=1, device_id=target, device_id_type=MESH)
@@ -122,32 +126,27 @@
     greet(dev(dz=-step_z))
     greet(dev(dy=1))
     greet(dev(dy=-1))
+    greet(dev(dy=2))
     greet(dev(dc=1))
-    greet({"grp": lax.rem(grp + 2 * zhi - 1 + 32, 32), "tp": tp})
+    greet(grp_at(1))
+    greet(grp_at(-1))
     owner = lax.div(x, 2) == c
     own_group = lax.rem(x, 2)
 
     @pl.loop(0, 32)
     def _(i):
         source_c = lax.rem(i, 2)
-        source_tp = (2 * source_c + lax.rem(zlo, 2)) * 2 + lax.div(zlo, 2)
+        source_tp = (2 * source_c + lax.div(zlo, 2)) * 2 + lax.rem(zlo + lax.div(zlo, 2), 2)
 
         @pl.when(jnp.logical_or(i != grp, source_tp != tp))
         def _():
             greet({"grp": i, "tp": source_tp})
 
-    to_self = (zlo == 2 * zhi + own_group).astype(jnp.int32)
-    pl.semaphore_wait(barrier, 9 + owner.astype(jnp.int32) * (64 - to_self))
+    to_self = (zlo == group_at(zhi, own_group)).astype(jnp.int32)
+    pl.semaphore_wait(barrier, 11 + owner.astype(jnp.int32) * (64 - to_self))
 
     def slab(group, tp_index):
         return rows_all.at[group, :, columns(tp_index)]
-
-    for copy in load_z:
-        copy.wait()
-    for group in range(2):
-        remote(z_source.at[group], slab(group, tp), ("z", group), dev(dz=4)).start()
-    for copy in load_own:
-        copy.wait()
 
     def spread(kind, tp_index):
         for group in range(2):
@@ -170,23 +169,19 @@
         for group in range(2):
             arrived(slab(group, tp_at(2, kind)), ("xr", kind, group))
 
-    spread(0, tp)
-    remote(
-        parents.at[3 * other], table.at[3 * zhi], ("halo",),
-        {"grp": lax.rem(grp + 1 - 2 * zhi + 32, 32), "tp": tp},
-    ).start()
-
-    buffers = (w_query, w_cross, w_out, w_cout)
+    buffers = (w_query, w_query, w_cross, w_out, w_cout)
+    widths = (slice(0, 512), slice(512, 768), slice(0, 256), slice(0, D), slice(0, D))
     slice_sent = is_source * zhi + (1 - is_source) * other
 
     def part(which, index, quarter, core, sub=None):
         rows = WEIGHT_ROWS[which]
-        start = quarter * (rows // 4) + core * (rows // 8)
         size = rows // 8
+        start = quarter * (rows // 4) + core * size
         if sub is not None:
-            size = rows // 16
+            size = size // 2
             start = start + sub * size
-        return buffers[which].at[index, pl.ds(pl.multiple_of(start, rows // 16), size), :]
+        there = pl.ds(pl.multiple_of(start, rows // 16), size)
+        return buffers[which].at[index, there, widths[which]]
 
     chain_copies = {}
 
@@ -212,7 +207,7 @@
             def _():
                 chain_copies[which, sub].start()
 
-            for way in (1, -1):
+            for way in (1, -1, 2):
                 remote(ref, ref, ("y", which, sub, way), dev(dy=way)).start()
 
     def quarter_at(dy):
@@ -222,51 +217,50 @@
         ref = part(which, other, quarter_at(dy), c)
         remote(ref, ref, ("core", which, dy), dev(dc=1)).start()
 
-    def y_relay(which):
-        for sub, way in ((0, 1), (1, -1)):
-            ref = part(which, other, quarter_at(-way), c, sub)
-            arrived(ref, ("y", which, sub, way))
-            remote(ref, ref, ("yr", which, sub), dev(dy=way)).start()
+    def y_middle(which):
         core_forward(which, 0)
+        for way in (1, -1, 2):
+            for sub in range(2):
+                arrived(part(which, other, quarter_at(-way), c, sub), ("y", which, sub, way))
+            core_forward(which, -way)
 
     def y_end(which):
-        for sub, way in ((1, 1), (0, -1)):
-            arrived(part(which, other, quarter_at(-way), c, sub), ("y", which, sub, way))
-            core_forward(which, -way)
-        for sub in range(2):
-            arrived(part(which, other, quarter_at(2), c, sub), ("yr", which, sub))
-        core_forward(which, 2)
-        for dy in (0, 1, -1, 2):
+        for dy in (0, 1, -1, -2):
             arrived(part(which, other, quarter_at(dy), 1 - c), ("core", which, dy))
-
-    for copy in load_query:
-        copy.wait()
-    chain_start(QUERY)
 
     def choose():
         for copy in load_table:
             copy.wait()
-        arrived(table.at[3 * zhi], ("halo",))
-        for group in range(2):
-            index = grp * 4 + 2 * zhi + group
-            first = pairs[2 * zhi + group, 0]
-            second = pairs[2 * zhi + group, 1]
-            chosen[group * 32 : group * 32 + 16, :] = jnp.where(
-                first == index - 1, table[group], table[group + 1]
+        arrived(table.at[0], ("halo", 1))
+        arrived(table.at[5], ("halo", -1))
+        for place_at in range(4):
+            group = group_at(zhi if place_at < 2 else other, place_at % 2)
+            index = grp * 4 + group
+            rows = place_at * 32
+            chosen[rows : rows + 16, :] = jnp.where(
+                pairs[group, 0] == index - 1, table[group], table[group + 1]
             )
-            chosen[group * 32 + 16 : group * 32 + 32, :] = jnp.where(
-                second == index + 1, table[group + 2], table[group + 1]
+            chosen[rows + 16 : rows + 32, :] = jnp.where(
+                pairs[group, 1] == index + 1, table[group + 2], table[group + 1]
             )
+        for copy in load_kv:
+            copy.wait()
+        kv_own[...] = jnp.dot(chosen[...], w_kv[...], preferred_element_type=F32).astype(BF)
+        remote(kv_own.at[64:128], kv_other, ("kv",), dev(dz=4)).start()
 
     def fold_slice(phase, index):
-        kv = jnp.dot(chosen[...], w_cross[index, :, 0:512], preferred_element_type=F32).astype(BF)
+        if phase == 0:
+            kv = kv_own[0:64, :]
+        else:
+            arrived(kv_other, ("kv",))
+            kv = kv_other[...]
         for head in range(2):
             key = kv[:, head * HD : (head + 1) * HD]
             value = kv[:, 256 + head * HD : 256 + (head + 1) * HD]
             for n in range(4):
                 cols = slice(n * 512, (n + 1) * 512)
                 left = lax.dot_general(
-                    key, w_cross[index, cols, 512 + head * HD : 512 + (head + 1) * HD],
+                    key, w_cross[index, cols, head * HD : (head + 1) * HD],
                     (((1,), (1,)), ((), ())), preferred_element_type=F32,
                 ) * (1.0 / math.sqrt(HD))
                 right = jnp.dot(
@@ -281,10 +275,8 @@
 
     def fold_start(phase):
         index = zhi if phase == 0 else other
-        base = sem_id("fold", phase, 0)
-        for extra in range(1, 8):
+        for extra in range(8):
             sem_id("fold", phase, extra)
-        del base
         for group in range(2):
             for side in range(2):
                 rows = pl.ds(pl.multiple_of(x * 128 + index * 64, 64), 64)
@@ -319,99 +311,133 @@
             values = rows_all[group, rows, :].astype(F32)
             hidden[group, rows, :] = norm_rows(values, scale, shift).astype(BF)
 
-    def attend(group):
+    def attend(group, s):
         mod = rows_all[group, ROWS:EXT, 0:256].astype(F32)
         frame = lax.div(lax.broadcasted_iota(jnp.int32, (1, ROWS), 1), P_SIZE).astype(F32)
         keep = (frame < mod[6:7]).astype(F32)
 
-        @pl.loop(0, 2)
-        def _(s):
-            for n in range(3):
-                cols = slice(n * 256, (n + 1) * 256)
-                qkv[:, cols] = jnp.dot(
-                    hidden[group], w_query[s, :, cols], preferred_element_type=F32
-                ).astype(BF)
-            for head in range(2):
-                cols = slice(head * HD, (head + 1) * HD)
-                query = qkv[:, cols]
-                key = qkv[:, 256 + head * HD : 256 + (head + 1) * HD]
-                value = qkv[:, 512 + head * HD : 512 + (head + 1) * HD]
-                scores = lax.dot_general(
-                    query, key, (((1,), (1,)), ((), ())), preferred_element_type=F32
-                ) * (1.0 / math.sqrt(HD))
-                weights = jnp.exp(scores) * keep
-                probs = (weights / jnp.sum(weights, axis=-1, keepdims=True)).astype(BF)
-                attn[s, :, cols] = jnp.dot(probs, value, preferred_element_type=F32).astype(BF)
+        for n in range(3):
+            cols = slice(n * 256, (n + 1) * 256)
+            qkv[:, cols] = jnp.dot(
+                hidden[group], w_query[s, :, cols], preferred_element_type=F32
+            ).astype(BF)
+        for head in range(2):
+            cols = slice(head * HD, (head + 1) * HD)
+            query = qkv[:, cols]
+            key = qkv[:, 256 + head * HD : 256 + (head + 1) * HD]
+            value = qkv[:, 512 + head * HD : 512 + (head + 1) * HD]
+            scores = lax.dot_general(
+                query, key, (((1,), (1,)), ((), ())), preferred_element_type=F32
+            ) * (1.0 / math.sqrt(HD))
+            weights = jnp.exp(scores) * keep
+            probs = (weights / jnp.sum(weights, axis=-1, keepdims=True)).astype(BF)
+            attn[group, s, :, cols] = jnp.dot(probs, value, preferred_element_type=F32).astype(BF)
 
     def project(group):
         for n in range(4):
             cols = slice(n * 512, (n + 1) * 512)
-            total = jnp.dot(attn[0], w_out[0, :, cols], preferred_element_type=F32)
-            total = total + jnp.dot(attn[1], w_out[1, :, cols], preferred_element_type=F32)
+            total = jnp.dot(attn[group, 0], w_out[0, :, cols], preferred_element_type=F32)
+            total = total + jnp.dot(attn[group, 1], w_out[1, :, cols], preferred_element_type=F32)
             branch_send[group, :, cols] = total.astype(BF)
-        src, dst = branch_send.at[group], branch_recv.at[x]
-        base = sem_id("branch", 0)
-        for index in range(1, 4):
-            sem_id("branch", index)
-        copy = pltpu.make_async_remote_copy(
-            src_ref=src, dst_ref=dst, send_sem=send_sem.at[sem_id("bs", group)],
-            recv_sem=recv_sem.at[base + x],
+    def branch_copy(group, half):
+        rows = pl.ds(half * 128, 128)
+        src, dst = branch_send.at[group, rows, :], branch_recv.at[x, rows, :]
+        for index in range(4):
+            sem_id("branch", half, index)
+        slot = sem_id("branch", half, 0) + x
+        return src, dst, slot, pltpu.make_async_remote_copy(
+            src_ref=src, dst_ref=dst, send_sem=send_sem.at[sem_id("bs", group, half)],
+            recv_sem=recv_sem.at[slot],
             device_id={"grp": grp, "tp": (2 * c + group) * 2 + zhi}, device_id_type=MESH,
         )
 
+    def branch_start(group, half):
+        src, dst, slot, copy = branch_copy(group, half)
+
         @pl.when(x == 2 * c + group)
         def _():
-            pltpu.make_async_copy(src, dst, recv_sem.at[base + x]).start()
+            pltpu.make_async_copy(src, dst, recv_sem.at[slot]).start()
 
         @pl.when(x != 2 * c + group)
         def _():
             copy.start()
 
-        guarded.append((x != 2 * c + group, copy))
-
+    def branch_sent(group, half):
+        copy = branch_copy(group, half)[3]
+
+        @pl.when(x != 2 * c + group)
+        def _():
+            copy.wait_send()
+
+    def ready(copies):
+        for copy in copies:
+            copy.wait()
+
+    ready(load_z)
+    for group in range(2):
+        remote(z_source.at[group], slab(group, tp), ("z", group), dev(dz=4)).start()
+    ready(load_own)
+    spread(0, tp)
+    remote(parents.at[3], table.at[0], ("halo", 1), grp_at(1)).start()
+    remote(parents.at[0], table.at[5], ("halo", -1), grp_at(-1)).start()
+    ready(load_cross)
+    chain_start(CROSS)
+    ready(load_cout)
+    chain_start(COUT)
+    ready(load_query)
+    chain_start(KEYS)
+    ready(load_out)
+    chain_start(VALUES)
+    chain_start(OUT)
+    choose()
     spread_relay(0)
-    chain_relay(QUERY)
+    chain_relay(CROSS)
+    chain_relay(COUT)
+    chain_relay(KEYS)
+    fold_slice(0, zhi)
+    fold_start(0)
     for group in range(2):
         arrived(slab(group, tp_at(0, 1)), ("z", group))
     spread(1, tp_at(0, 1))
-    for copy in load_out + load_cross + load_cout:
-        copy.wait()
-    chain_start(OUT)
-    chain_start(CROSS)
-    chain_start(COUT)
+    chain_relay(VALUES)
+    chain_relay(OUT)
+    y_middle(CROSS)
+    y_middle(COUT)
+    spread_relay(1)
+    y_middle(KEYS)
+    y_end(CROSS)
+    y_end(COUT)
+    fold_slice(1, other)
+    fold_start(1)
+    spread_end(0)
+    spread_end(1)
+    normalise(0)
+    y_middle(VALUES)
+    normalise(1)
+    attend(0, zhi)
+    y_middle(OUT)
+    attend(1, zhi)
+    y_end(KEYS)
+    y_end(VALUES)
+    attend(0, other)
+    y_end(OUT)
+    project(0)
+    branch_start(0, 0)
+    attend(1, other)
+    project(1)
+    branch_start(1, 0)
+    branch_sent(0, 0)
+    branch_start(0, 1)
+    branch_sent(1, 0)
+    branch_start(1, 1)
     blocks[...] = (
         lax.div(lax.broadcasted_iota(jnp.int32, (512, 512), 0), 32)
         == lax.div(lax.broadcasted_iota(jnp.int32, (512, 512), 1), 32)
     ).astype(F32).astype(BF)
-    choose()
-    fold_slice(0, zhi)
-    spread_relay(1)
-    y_relay(QUERY)
-    spread_end(0)
-    spread_end(1)
-    fold_start(0)
-    normalise(0)
-    chain_relay(OUT)
-    normalise(1)
-    y_end(QUERY)
-    y_relay(OUT)
-    attend(0)
-    y_end(OUT)
-    chain_relay(CROSS)
-    project(0)
-    attend(1)
-    project(1)
-    y_relay(CROSS)
-    chain_relay(COUT)
-    y_end(CROSS)
-    y_relay(COUT)
-    y_end(COUT)
-    fold_slice(1, other)
-    fold_start(1)
 
     def final_copy(i):
         near, far = lax.div(i, 8), lax.rem(i, 8)
-        target = (2 * zhi + own_group) * 8 + near
+        target = group_at(zhi, own_group) * 8 + near
         src = result.at[pl.ds(pl.multiple_of(near * 32, 32), 32), columns(far)]
         dst = out.at[grp]
         return target, far, src, dst, pltpu.make_async_remote_copy(
@@ -421,31 +447,32 @@
 
     @pl.when(owner)
     def _():
-        for index in range(4):
-            arrived(branch_recv.at[index], ("branch", 0), index)
         mod = rows_all[own_group, ROWS:EXT, :].astype(F32)
         gate1, shift2, scale2, gate2 = mod[2:3], mod[3:4], mod[4:5], mod[5:6]
-
-        @pl.loop(0, ROWS // 32)
-        def _(i):
-            rows = pl.ds(pl.multiple_of(i * 32, 32), 32)
-            total = branch_recv[0, rows, :].astype(F32)
-            for index in range(1, 4):
-                total = total + branch_recv[index, rows, :].astype(F32)
-            value = (rows_all[own_group, rows, :].astype(F32) + gate1 * total).astype(BF)
-            x_one[rows, :] = value
-            hidden[0, rows, :] = norm_rows(value.astype(F32), scale2, shift2).astype(BF)
-
-        for phase in range(2):
-            index = zhi if phase == 0 else other
-            for source in range(4):
-                rows = pl.ds(pl.multiple_of(source * 128 + index * 64, 64), 64)
-                for side in range(2):
-                    arrived(fold.at[side, rows, :], ("fold", phase, 0), source * 2 + side)
-
-        @pl.loop(0, 2)
-        def _(i):
-            rows = pl.ds(pl.multiple_of(i * 128, 128), 128)
+        for half in range(2):
+            for index in range(4):
+                arrived(
+                    branch_recv.at[index, pl.ds(half * 128, 128), :], ("branch", half, 0), index
+                )
+
+            @pl.loop(0, 4)
+            def _(i):
+                rows = pl.ds(pl.multiple_of(half * 128 + i * 32, 32), 32)
+                total = branch_recv[0, rows, :].astype(F32)
+                for index in range(1, 4):
+                    total = total + branch_recv[index, rows, :].astype(F32)
+                value = (rows_all[own_group, rows, :].astype(F32) + gate1 * total).astype(BF)
+                x_one[rows, :] = value
+                hidden[0, rows, :] = norm_rows(value.astype(F32), scale2, shift2).astype(BF)
+
+            for phase in range(2 if half == 0 else 0):
+                index = zhi if phase == 0 else other
+                for source in range(4):
+                    rows = pl.ds(pl.multiple_of(source * 128 + index * 64, 64), 64)
+                    for side in range(2):
+                        arrived(fold.at[side, rows, :], ("fold", phase, 0), source * 2 + side)
+
+            rows = pl.ds(half * 128, 128)
             scores = lax.dot_general(
                 hidden[0, rows, :], fold[0], (((1,), (1,)), ((), ())), preferred_element_type=F32
             )
@@ -459,7 +486,7 @@
                     x_one[rows, cols].astype(F32) + gate2[:, cols] * branch
                 ).astype(BF)
 
-            @pl.loop(i * 32, i * 32 + 32)
+            @pl.loop(half * 32, half * 32 + 32)
             def _(j):
                 target, far, src, dst, copy = final_copy(j)
                 mine = jnp.logical_and(target == grp, far == tp)
@@ -479,6 +506,9 @@
         @pl.when(condition)
         def _():
             copy.wait_send()
+
+    branch_sent(0, 1)
+    branch_sent(1, 1)
 
     @pl.when(owner)
     def _():
@@ -518,14 +548,17 @@
             pltpu.VMEM((2, EXT, D), BF),
             pltpu.VMEM((2, EXT, 256), BF),
             pltpu.VMEM((2, D, 768), BF),
-            pltpu.VMEM((2, D, 768), BF),
+            pltpu.VMEM((2, D, 256), BF),
             pltpu.VMEM((2, 2 * HD, D), BF),
             pltpu.VMEM((2, 2 * HD, D), BF),
-            pltpu.VMEM((4, P_SIZE, D), BF),
-            pltpu.VMEM((64, D), BF),
+            pltpu.VMEM((D, 512), BF),
+            pltpu.VMEM((6, P_SIZE, D), BF),
+            pltpu.VMEM((128, D), BF),
+            pltpu.VMEM((128, 512), BF),
+            pltpu.VMEM((64, 512), BF),
             pltpu.VMEM((2, ROWS, D), BF),
             pltpu.VMEM((ROWS, 768), BF),
-            pltpu.VMEM((2, ROWS, 2 * HD), BF),
+            pltpu.VMEM((2, 2, ROWS, 2 * HD), BF),
             pltpu.VMEM((2, ROWS, D), BF),
             pltpu.VMEM((4, ROWS, D), BF),
             pltpu.VMEM((2, 2, 2, 64, D), BF),

time: 155 us -> 135 us (0.87)
  Pallas kernels: 143 us -> 122 us
    pallas_call x1, Pallas kernels: 143 us -> 122 us  [on_device(): pl.pallas_call(kernel, out_shape=jax.ShapeDtypeStruct((32, 32, 256), BF),...]
where the time goes in v2:
time: 135 us; the launch traced here: 134 us
  Pallas kernels  122 us (90%)
  local copies, waits for them, and re-layouts  9.56 us (7%)
  other arithmetic  2.35 us (2%)
    pallas_call x1, Pallas kernels, on_device(): pl.pallas_call(kernel, out_shape=jax.ShapeDtypeStruct((32, 32, 256), BF),...  122 us
    unnamed x9, local copies, waits for them, and re-layouts  5.72 us

profile of v2, /device:TPU:127, one launch (start us, length us, event | category | flops | bytes accessed | tf_op | source)
XLA Modules:
  0.0 133.9 jit_solution(18271761409093925548)
XLA Ops:
  0.0 0.0 copy-start
  0.0 0.0 copy-start.2
  0.0 0.8 convert_element_type.12
  0.8 0.7 convert_element_type.15
  1.5 0.1 pad.2.clone
  1.6 1.3 copy.21.pairs
  3.0 0.1 multiply_cosine_fusion
  3.1 0.1 broadcast_in_dim.4
  3.2 0.0 copy-done
  3.2 0.2 convolution_convert_fusion
  3.4 0.7 maximum_maximum_fusion.modx
  4.1 0.0 copy-start.1
  4.1 2.5 %copy.23 = bf16[2048,2,128]{2,0,1:T(8,128)(2,1)} copy(bf16[2048,2,128]{2,1,0:T(2,128)(2,1)} %param.19) | data formatting | bytes 2097152 | tf_op args[8]
  6.6 0.0 copy-done.2
  6.6 1.6 %copy.19 = bf16[2,2,2048,128]{3,2,1,0:T(8,128)(2,1)} copy(bf16[2,2,2048,128]{3,1,0,2:T(2,128)(2,1)S(1)} %bitcast.19) | data formatting | bytes 4194304 | tf_op jit(solution)/shard_map/transpose | solution.py:539
  8.2 0.0 copy-done.1
  8.2 2.1 %copy.18 = bf16[3,2,2048,128]{3,2,1,0:T(8,128)(2,1)} copy(bf16[3,2,2048,128]{3,1,0,2:T(2,128)(2,1)S(1)} %bitcast.18) | data formatting | bytes 6291456 | tf_op jit(solution)/shard_map/transpose | solution.py:538
  10.3 121.7 %dit_block.1 = bf16[32,32,256]{2,1,0:T(8,128)(2,1)} custom-call(bf16[4,256,256]{2,1,0:T(8,128)(2,1)} %bitcast.23, bf16[4,16,256]{2,1,0:T(8,128)(2,1)} %maximum_maximum_fusion.modx, bf16[4,16,2048]{2,1,0:T(8,128)(2,1)} %parents.1, bf16[6,2048,128]{2,1,0:T(8,128)(2,1)} %bitcast.15, bf16[4,2048,128]{2,1,0:T(8,128)(2,1)} %bitcast.16, ...), custom_call_target="tpu_custom_call" | custom-call | tf_op jit(solution)/shard_map/dit_block/pallas_call | solution.py:542
  132.0 1.9 %copy.25 = bf16[32,2,16,256]{3,2,1,0:T(8,128)(2,1)} copy(bf16[32,2,16,256]{3,2,1,0:T(8,128)(2,1)} %bitcast.20) | data formatting | bytes 1048576
  (3 shorter events, 0.0 us)
Async XLA Ops:
  0.0 3.2 %copy-start = (bf16[256,6,256]{2,0,1:T(8,128)(2,1)S(1)}, bf16[256,6,256]{2,0,1:T(8,128)(2,1)}, u32[]{:S(2)}) copy-start(bf16[256,6,256]{2,0,1:T(8,128)(2,1)} %param.16) | copy-start | bytes 2359300
  0.0 6.6 %copy-start.2 = (bf16[2048,2,2,128]{3,2,1,0:T(2,128)(2,1)S(1)}, bf16[2048,2,2,128]{3,2,1,0:T(2,128)(2,1)}, u32[]{:S(2)}) copy-start(bf16[2048,2,2,128]{3,2,1,0:T(2,128)(2,1)} %param.20) | copy-start | bytes 6291460
  4.1 4.1 %copy-start.1 = (bf16[2048,3,2,128]{3,2,1,0:T(2,128)(2,1)S(1)}, bf16[2048,3,2,128]{3,2,1,0:T(2,128)(2,1)}, u32[]{:S(2)}) copy-start(bf16[2048,3,2,128]{3,2,1,0:T(2,128)(2,1)} %param.17) | copy-start | bytes 9437188

commit v3 on v2

--- a/solution.py
+++ b/solution.py
@@ -394,13 +394,13 @@
     chain_relay(CROSS)
     chain_relay(COUT)
     chain_relay(KEYS)
-    fold_slice(0, zhi)
-    fold_start(0)
+    chain_relay(VALUES)
     for group in range(2):
         arrived(slab(group, tp_at(0, 1)), ("z", group))
     spread(1, tp_at(0, 1))
-    chain_relay(VALUES)
     chain_relay(OUT)
+    fold_slice(0, zhi)
+    fold_start(0)
     y_middle(CROSS)
     y_middle(COUT)
     spread_relay(1)

time: 135 us -> 136 us (level)
  the two profiles are of different devices: /device:TPU:127 before, /device:TPU:31 now
where the time goes in v3:
time: 136 us
  Pallas kernels  124 us (91%)
  local copies, waits for them, and re-layouts  9.56 us (7%)
  other arithmetic  2.35 us (2%)
    pallas_call x1, Pallas kernels, on_device(): pl.pallas_call(kernel, out_shape=jax.ShapeDtypeStruct((32, 32, 256), BF),...  124 us
    unnamed x9, local copies, waits for them, and re-layouts  5.72 us

profile of v3, /device:TPU:31, one launch (start us, length us, event | category | flops | bytes accessed | tf_op | source)
XLA Modules:
  0.0 135.7 jit_solution(2122592592840881176)
XLA Ops:
  0.0 0.0 copy-start
  0.0 0.0 copy-start.2
  0.0 0.8 convert_element_type.12
  0.8 0.7 convert_element_type.15
  1.5 0.1 pad.2.clone
  1.6 1.3 copy.21.pairs
  3.0 0.1 multiply_cosine_fusion
  3.1 0.1 broadcast_in_dim.4
  3.2 0.0 copy-done
  3.2 0.2 convolution_convert_fusion
  3.4 0.7 maximum_maximum_fusion.modx
  4.1 0.0 copy-start.1
  4.1 2.5 %copy.23 = bf16[2048,2,128]{2,0,1:T(8,128)(2,1)} copy(bf16[2048,2,128]{2,1,0:T(2,128)(2,1)} %param.19) | data formatting | bytes 2097152 | tf_op args[8]
  6.6 0.0 copy-done.2
  6.6 1.6 %copy.19 = bf16[2,2,2048,128]{3,2,1,0:T(8,128)(2,1)} copy(bf16[2,2,2048,128]{3,1,0,2:T(2,128)(2,1)S(1)} %bitcast.19) | data formatting | bytes 4194304 | tf_op jit(solution)/shard_map/transpose | solution.py:539
  8.2 0.0 copy-done.1
  8.2 2.1 %copy.18 = bf16[3,2,2048,128]{3,2,1,0:T(8,128)(2,1)} copy(bf16[3,2,2048,128]{3,1,0,2:T(2,128)(2,1)S(1)} %bitcast.18) | data formatting | bytes 6291456 | tf_op jit(solution)/shard_map/transpose | solution.py:538
  10.3 123.5 %dit_block.1 = bf16[32,32,256]{2,1,0:T(8,128)(2,1)} custom-call(bf16[4,256,256]{2,1,0:T(8,128)(2,1)} %bitcast.23, bf16[4,16,256]{2,1,0:T(8,128)(2,1)} %maximum_maximum_fusion.modx, bf16[4,16,2048]{2,1,0:T(8,128)(2,1)} %parents.1, bf16[6,2048,128]{2,1,0:T(8,128)(2,1)} %bitcast.15, bf16[4,2048,128]{2,1,0:T(8,128)(2,1)} %bitcast.16, ...), custom_call_target="tpu_custom_call" | custom-call | tf_op jit(solution)/shard_map/dit_block/pallas_call | solution.py:542
  133.8 1.9 %copy.25 = bf16[32,2,16,256]{3,2,1,0:T(8,128)(2,1)} copy(bf16[32,2,16,256]{3,2,1,0:T(8,128)(2,1)} %bitcast.20) | data formatting | bytes 1048576
  (3 shorter events, 0.0 us)
Async XLA Ops:
  0.0 3.2 %copy-start = (bf16[256,6,256]{2,0,1:T(8,128)(2,1)S(1)}, bf16[256,6,256]{2,0,1:T(8,128)(2,1)}, u32[]{:S(2)}) copy-start(bf16[256,6,256]{2,0,1:T(8,128)(2,1)} %param.16) | copy-start | bytes 2359300
  0.0 6.6 %copy-start.2 = (bf16[2048,2,2,128]{3,2,1,0:T(2,128)(2,1)S(1)}, bf16[2048,2,2,128]{3,2,1,0:T(2,128)(2,1)}, u32[]{:S(2)}) copy-start(bf16[2048,2,2,128]{3,2,1,0:T(2,128)(2,1)} %param.20) | copy-start | bytes 6291460
  4.1 4.1 %copy-start.1 = (bf16[2048,3,2,128]{3,2,1,0:T(2,128)(2,1)S(1)}, bf16[2048,3,2,128]{3,2,1,0:T(2,128)(2,1)}, u32[]{:S(2)}) copy-start(bf16[2048,3,2,128]{3,2,1,0:T(2,128)(2,1)} %param.17) | copy-start | bytes 9437188
